TPU v7x, 32 devices: a whole 2x2x4 slice. The times are simulated.
32 devices in a mesh: tile: 8 (over z, x), mode: 4 (over y, core).
Axes of the slice: x: 2, y: 2, z: 4, core: 2. Of those that a mesh axis runs over, the one named last changes fastest.
Arguments:
- obj_x: float32 [2, 256, 512], P(None, 'tile', 'mode'), may hold values from -6 to 6
- dual_u: float32 [2, 256, 512], P(None, 'tile', 'mode'), may hold values from -6 to 6
- probes: float32 [4, 2, 256, 256], P('mode'), may hold values from -4 to 4
- intensity: float32 [8, 256, 256], P('tile'), may hold values from 0.1 to 4
- corners: int32 [2, 8], replicated, may hold values from 0 to 256, as said below
- owner: int32 [8], replicated, may hold values from 0 to 7, as said below
- w_in: bfloat16 [9, 48, 2], replicated, may hold values from -1.5 to 1.5
- b_in: float32 [48], replicated, may hold values from -3 to 3
- w_down: bfloat16 [4, 48, 48], replicated, may hold values from -0.4375 to 0.4375
- b_down: float32 [48], replicated, may hold values from -3 to 3
- w_mid: bfloat16 [9, 48, 48], replicated, may hold values from -0.3125 to 0.3125
- b_mid: float32 [48], replicated, may hold values from -3 to 3
- w_out: bfloat16 [9, 2, 48], replicated, may hold values from -0.3125 to 0.3125
- b_out: float32 [2], replicated, may hold values from -3 to 3
Outputs:
- obj_next: float32 [2, 256, 512], P(None, 'tile', 'mode')
- aux_next: float32 [2, 256, 512], P(None, 'tile', 'mode')
- dual_next: float32 [2, 256, 512], P(None, 'tile', 'mode')
- misfit: float32 [8], P('tile')
Inputs may be any that keep to these rules, and one draw needn't show every extreme that they name: Row corners lie in 0 to 0 and column corners in 0 to 256; the upper ends are reached in every draw. Every index of tile owns between 1 and 1 positions and some owns exactly 1; of the positions of one owner at most 1 have patterns that touch one block of 32 object rows held by one index of tile, and in every draw some owner and block reach 1.
All inputs are finite; a program needn't handle non-finite values.
Results may differ from a plain program's by a relative error of at most 0.01.
Values may be sent and summed in bfloat16 or wider, within the bound.
A program may use at most 128 MiB of HBM per device.

v0:
```python
import math

import jax
import jax.numpy as jnp
from jax import lax
from jax.sharding import PartitionSpec as P

HALO = 6


rho_weight = 2.0
floor_level = 0.25


def extended_2(value, sides, width):
    for axis, dim in sides:
        count, length = (lax.axis_size(axis), value.shape[dim])
        up = [(i, (i + 1) % count) for i in range(count - 1)]
        down = [(j, i) for i, j in up]
        last = lax.slice_in_dim(value, length - width, length, axis=dim)
        first = lax.slice_in_dim(value, 0, width, axis=dim)
        before = lax.ppermute(last, axis, up)
        after = lax.ppermute(first, axis, down)
        value = jnp.concatenate([before, value, after], axis=dim)
    return value


def conv_block(act, weight):
    height = act.shape[1]
    width = act.shape[2]
    padded = jnp.pad(act, ((0, 0), (1, 1), (1, 1)))
    total = jnp.zeros((weight.shape[1], height, width), jnp.float32)
    for tap in range(9):
        shift_row = tap // 3
        shift_col = tap % 3
        window = padded[:, shift_row : shift_row + height, shift_col : shift_col + width]
        total = total + jnp.einsum(
            "oc,chw->ohw", weight[tap], window, preferred_element_type=jnp.float32
        )
    return total


def dft_tables(length, sign):
    grid = (
        jnp.arange(length, dtype=jnp.int32)[:, None]
        * jnp.arange(length, dtype=jnp.int32)[None, :]
        % length
    )
    angle = 2.0 * math.pi / length * grid.astype(jnp.float32)
    factor = 1.0 / math.sqrt(length)
    return (jnp.cos(angle) * factor, sign * jnp.sin(angle) * factor)


def left_product(table, values):
    return jnp.einsum("ab,nbc->nac", table, values, precision=lax.Precision.HIGHEST)


def right_product(values, table):
    return jnp.einsum("nab,bc->nac", values, table, precision=lax.Precision.HIGHEST)


def left_apply(table_re, table_im, real_x, imag_x):
    real_out = left_product(table_re, real_x) - left_product(table_im, imag_x)
    imag_out = left_product(table_re, imag_x) + left_product(table_im, real_x)
    return (real_out, imag_out)


def right_apply(real_x, imag_x, table_re, table_im):
    real_out = right_product(real_x, table_re) - right_product(imag_x, table_im)
    imag_out = right_product(real_x, table_im) + right_product(imag_x, table_re)
    return (real_out, imag_out)


def window_plan(
    index_list,
    pos_count,
    first_strip,
    last_strip,
    row_corner,
    rows_dev,
    strips_per,
    tile_count,
    pair_most,
):
    live = index_list < pos_count
    where_pos = jnp.minimum(index_list, pos_count - 1)
    own_first = first_strip[where_pos]
    own_last = last_strip[where_pos]
    strip_of = own_first[:, None] + jnp.arange(strips_per, dtype=jnp.int32)[None, :]
    order = jnp.arange(index_list.shape[0], dtype=jnp.int32)
    before = (order[None, None, :] < order[:, None, None]) & live[None, None, :]
    hits = (
        before
        & (own_first[None, None, :] <= strip_of[:, :, None])
        & (own_last[None, None, :] >= strip_of[:, :, None])
    )
    rank_at = jnp.sum(hits.astype(jnp.int32), axis=2)
    in_use = live[:, None] & (strip_of <= own_last[:, None])
    strip_safe = jnp.minimum(strip_of, tile_count - 1)
    rank_safe = jnp.minimum(rank_at, pair_most - 1)
    offsets = row_corner[where_pos] - own_first * rows_dev
    return (live, strip_of, rank_at, in_use, strip_safe, rank_safe, offsets)


def send_slots(touches, owner, indices, pair_most, slot_count, pos_count):
    earlier_same = (
        (owner[:, None] == owner[None, :])
        & touches[None, :]
        & (indices[None, :] < indices[:, None])
    )
    send_rank = jnp.sum(earlier_same.astype(jnp.int32), axis=1)
    send_target = jnp.where(touches, owner * pair_most + send_rank, slot_count)
    send_table = (
        jnp.full((slot_count,), pos_count, jnp.int32).at[send_target].set(indices, mode="drop")
    )
    return (jnp.minimum(send_table, pos_count - 1), send_table < pos_count)


def per_device(
    obj_x,
    dual_u,
    probes,
    intensity,
    corners,
    owner,
    w_in,
    b_in,
    w_down,
    b_down,
    w_mid,
    b_mid,
    w_out,
    b_out,
):
    tile_id = lax.axis_index("tile")
    mode_id = lax.axis_index("mode")
    tile_count = lax.axis_size("tile")
    mode_count = lax.axis_size("mode")
    rows_dev = obj_x.shape[1]
    cols_dev = obj_x.shape[2]
    width_all = cols_dev * mode_count
    height_all = rows_dev * tile_count
    patch = probes.shape[-1]
    own_most = intensity.shape[0]
    pos_count = owner.shape[0]
    chans = w_in.shape[1]
    bands = max(1, (height_all - patch - rows_dev) // (patch + 2 * rows_dev))
    pair_most = (own_most + bands - 1) // bands
    slot_count = tile_count * pair_most
    strips_per = patch // rows_dev + 1
    row_corner = corners[0]
    col_corner = corners[1]
    first_strip = row_corner // rows_dev
    last_strip = (row_corner + patch - 1) // rows_dev
    indices = jnp.arange(pos_count, dtype=jnp.int32)
    touches = (first_strip <= tile_id) & (last_strip >= tile_id)
    is_mine = owner == tile_id
    mine_rank = jnp.cumsum(is_mine.astype(jnp.int32)) - 1
    own_index = (
        jnp.full((own_most,), pos_count, jnp.int32)
        .at[jnp.where(is_mine, mine_rank, own_most)]
        .set(indices, mode="drop")
    )
    obj_low = obj_x.astype(jnp.bfloat16)
    strip_full = lax.all_gather(obj_low, "mode", axis=2, tiled=True)
    anchor = jnp.zeros((), jnp.int32)
    den_plane = jnp.full((), 2, jnp.int32)
    table_re, table_im = dft_tables(patch, -1.0)
    all_probes = lax.all_gather(probes, "mode", axis=0, tiled=True)
    all_re = all_probes[:, 0]
    all_im = all_probes[:, 1]
    probe_power = jnp.sum(all_re * all_re + all_im * all_im, axis=0)
    earlier = (owner[:, None] == owner[None, :]) & (indices[None, :] < indices[:, None])
    pos_rank = jnp.sum(earlier.astype(jnp.int32), axis=1)
    dealt = touches & (pos_rank % mode_count == mode_id)
    slot_pos, slot_live = send_slots(dealt, owner, indices, pair_most, slot_count, pos_count)
    local_most = (own_most + mode_count - 1) // mode_count
    local_rank = mode_id + mode_count * jnp.arange(local_most, dtype=jnp.int32)
    rank_safe_local = jnp.minimum(local_rank, own_most - 1)
    local_index = jnp.where(local_rank < own_most, own_index[rank_safe_local], pos_count)
    plan = window_plan(
        local_index,
        pos_count,
        first_strip,
        last_strip,
        row_corner,
        rows_dev,
        strips_per,
        tile_count,
        pair_most,
    )
    local_live = plan[0]
    starts = col_corner[slot_pos] + 0

    def take(start):
        return lax.dynamic_slice_in_dim(strip_full, start, patch, 2)

    cut = jax.vmap(take)(starts)
    arrived = lax.all_to_all(
        cut.reshape(tile_count, pair_most, 2, rows_dev * patch),
        "tile",
        split_axis=0,
        concat_axis=0,
        tiled=True,
    )
    strip_safe = plan[4]
    rank_safe = plan[5]
    offsets = plan[6]
    count = offsets.shape[0]
    blocks = arrived.reshape(tile_count, pair_most, 2, rows_dev, patch)
    picked = blocks[strip_safe, rank_safe]
    tall = jnp.transpose(picked, (0, 2, 1, 3, 4)).reshape(count, 2, strips_per * rows_dev, patch)

    def crop(block, offset):
        return lax.dynamic_slice_in_dim(block, offset, patch, 1)

    patches = jax.vmap(crop)(tall, offsets)
    obj_re = patches[:, 0].astype(jnp.float32)[:, None]
    obj_im = patches[:, 1].astype(jnp.float32)[:, None]
    wave_re = (all_re[None] * obj_re - all_im[None] * obj_im).reshape(
        local_most * mode_count, patch, patch
    )
    wave_im = (all_re[None] * obj_im + all_im[None] * obj_re).reshape(
        local_most * mode_count, patch, patch
    )
    far_re, far_im = left_apply(table_re, table_im, wave_re, wave_im)
    far_re, far_im = right_apply(far_re, far_im, table_re, table_im)
    far_re = far_re.reshape(local_most, mode_count, patch, patch)
    far_im = far_im.reshape(local_most, mode_count, patch, patch)
    power_all = jnp.sum(far_re * far_re + far_im * far_im, axis=1)
    measured = jnp.sqrt(intensity[rank_safe_local])
    errors = jnp.mean((jnp.sqrt(power_all) - measured) ** 2, axis=(1, 2)) * local_live.astype(
        jnp.float32
    )
    misfit_local = jnp.zeros((own_most,), jnp.float32).at[local_rank].set(errors, mode="drop")
    misfit = lax.psum(misfit_local, "mode")
    scale = (measured / jnp.sqrt(jnp.maximum(power_all, floor_level)))[:, None]
    scaled_re = (far_re * scale).reshape(local_most * mode_count, patch, patch)
    scaled_im = (far_im * scale).reshape(local_most * mode_count, patch, patch)
    back_re, back_im = left_apply(table_re, -table_im, scaled_re, scaled_im)
    back_re, back_im = right_apply(back_re, back_im, table_re, -table_im)
    back_re = back_re.reshape(local_most, mode_count, patch, patch)
    back_im = back_im.reshape(local_most, mode_count, patch, patch)
    grad_re = (
        (all_re[None] * back_re + all_im[None] * back_im).astype(jnp.bfloat16).astype(jnp.float32)
    )
    grad_im = (
        (all_re[None] * back_im - all_im[None] * back_re).astype(jnp.bfloat16).astype(jnp.float32)
    )
    grad_sum = jnp.stack([jnp.sum(grad_re, axis=1), jnp.sum(grad_im, axis=1)], axis=1)
    probe_pad = jnp.pad(probe_power, ((rows_dev, rows_dev), (0, 0)))
    strip_of = plan[1]
    rank_at = plan[2]
    in_use = plan[3]
    offsets = plan[6]
    count = offsets.shape[0]
    tall = jnp.zeros((count, 2, strips_per * rows_dev, patch), grad_sum.dtype)

    def place(block, piece, offset):
        return lax.dynamic_update_slice_in_dim(block, piece, offset, 1)

    tall = jax.vmap(place)(tall, grad_sum, offsets)
    blocks = jnp.transpose(tall.reshape(count, 2, strips_per, rows_dev, patch), (0, 2, 1, 3, 4))
    target = jnp.where(in_use, strip_of * pair_most + rank_at, slot_count).reshape(-1)
    buffer = jnp.zeros((slot_count, 2, rows_dev * patch), grad_sum.dtype)
    buffer = buffer.at[target].set(
        blocks.reshape(count * strips_per, 2, rows_dev * patch), mode="drop"
    )
    back_pieces = lax.all_to_all(
        buffer.reshape(tile_count, pair_most, 2, rows_dev * patch),
        "tile",
        split_axis=0,
        concat_axis=0,
        tiled=True,
    )
    den_gate = jnp.ones((), jnp.float32)
    flat = back_pieces.reshape(slot_count, 2, rows_dev, patch)

    def add_slot(slot_no, acc):
        where_pos = slot_pos[slot_no]
        alive = slot_live[slot_no].astype(jnp.float32)
        col = col_corner[where_pos]
        piece = flat[slot_no] * alive
        row_start = tile_id * rows_dev - row_corner[where_pos] + rows_dev
        weight_rows = lax.dynamic_slice_in_dim(probe_pad, row_start, rows_dev, 0) * (
            alive * den_gate
        )
        old_num = lax.dynamic_slice(acc, (anchor, anchor, col + 0), (2, rows_dev, patch))
        acc = lax.dynamic_update_slice(acc, old_num + piece, (anchor, anchor, col + 0))
        old_den = lax.dynamic_slice(acc, (den_plane, anchor, col), (1, rows_dev, patch))
        return lax.dynamic_update_slice(acc, old_den + weight_rows[None], (den_plane, anchor, col))

    start_acc = jnp.zeros((3, rows_dev, width_all), jnp.float32)
    acc_rows = lax.fori_loop(0, slot_count, add_slot, start_acc)
    totals = lax.psum_scatter(acc_rows, "mode", scatter_dimension=2, tiled=True)
    base = obj_x + dual_u
    extended = extended_2(base.astype(jnp.bfloat16), (("tile", 1), ("mode", 2)), HALO)
    ext_rows = rows_dev + 2 * HALO
    ext_cols = cols_dev + 2 * HALO
    row_ids = tile_id * rows_dev - HALO + jnp.arange(ext_rows, dtype=jnp.int32)
    col_ids = mode_id * cols_dev - HALO + jnp.arange(ext_cols, dtype=jnp.int32)
    row_inside = (row_ids >= 0) & (row_ids < height_all)
    col_inside = (col_ids >= 0) & (col_ids < width_all)
    fine_mask = (row_inside[:, None] & col_inside[None, :]).astype(jnp.float32)
    coarse_mask = fine_mask[::2, ::2]
    first_map = (jax.nn.relu(conv_block(extended, w_in) + b_in[:, None, None]) * fine_mask).astype(
        jnp.bfloat16
    )
    pairs = first_map.reshape(chans, ext_rows // 2, 2, ext_cols // 2, 2)
    down_kernel = w_down.reshape(2, 2, chans, chans)
    coarse = jnp.einsum("ijoc,chiwj->ohw", down_kernel, pairs, preferred_element_type=jnp.float32)
    second_map = (jax.nn.relu(coarse + b_down[:, None, None]) * coarse_mask).astype(jnp.bfloat16)
    third_map = jax.nn.relu(conv_block(second_map, w_mid) + b_mid[:, None, None]).astype(
        jnp.bfloat16
    )
    upsampled = jnp.repeat(jnp.repeat(third_map.astype(jnp.float32), 2, axis=1), 2, axis=2)
    fourth_map = (upsampled * fine_mask + first_map.astype(jnp.float32)).astype(jnp.bfloat16)
    denoised = conv_block(fourth_map, w_out) + b_out[:, None, None]
    center = denoised[:, HALO : HALO + rows_dev, HALO : HALO + cols_dev]
    aux_next = base - center
    obj_next = (totals[0:2] + rho_weight * (aux_next - dual_u)) / (totals[2] + rho_weight)
    dual_next = dual_u + obj_next - aux_next
    return (obj_next, aux_next, dual_next, misfit)


def solution(mesh):
    return jax.shard_map(
        per_device,
        mesh=mesh,
        in_specs=(
            P(None, "tile", "mode"),
            P(None, "tile", "mode"),
            P("mode", None, None, None),
            P("tile", None, None),
            P(),
            P(),
            P(),
            P(),
            P(),
            P(),
            P(),
            P(),
            P(),
            P(),
        ),
        out_specs=(
            P(None, "tile", "mode"),
            P(None, "tile", "mode"),
            P(None, "tile", "mode"),
            P("tile"),
        ),
        check_vma=False,
    )
```

profile of v0, /device:TPU:0, one launch (start us, length us, event | category | flops | bytes accessed | tf_op | source)
XLA Modules:
  0.0 284.7 jit_solution(2205363872303452296)
XLA Ops:
  8.0 4.8 %collective-permute-start = (bf16[2,6,128]{2,0,1:T(2,128)(2,1)S(1)}, bf16[2,6,128]{2,0,1:T(2,128)(2,1)S(1)}, u32[]{:S(2)}, u32[]{:S(2)}) collective-permute-start(bf16[2,6,128]{2,0,1:T(2,128)(2,1)S(1)} %get-tuple-element.348), channel_id=1, source_target_pairs={{0,4},{4,8},{8,12},{12,16},{16,20},{20,24},{24,28},{1,5},{5,9},{9,... | collective-permute-start | bytes 9224 | tf_op jit(solution)/shard_map/ppermute | solution.py:22
  12.9 1.3 collective-permute-start.1
  20.3 5.3 %all_gather.7 = bf16[2,32,512]{2,1,0:T(8,128)(2,1)S(1)} all-gather(bf16[2,32,128]{2,1,0:T(8,128)(2,1)S(1)} %convert_element_type.122), channel_id=1, replica_groups=mesh['tile'=8,'mode'=4] {'mode'}, dimensions={2}, use_global_device_ids=true | all-gather | bytes 81920 | tf_op jit(solution)/shard_map/all_gather | solution.py:165
  25.7 2.7 gather_fusion.1
  29.7 7.0 %all-to-all-start = ((bf16[8,1,2,8192]{3,2,1,0:T(2,128)(2,1)}), bf16[8,1,2,8192]{3,2,1,0:T(2,128)(2,1)}, u32[]{:S(2)}, u32[]{:S(2)}) async-start(bf16[8,1,2,8192]{3,2,1,0:T(2,128)(2,1)} %reshape.693), calls=%async_computation | async-start | bytes 524288 | tf_op jit(solution)/shard_map/all_to_all | solution.py:199
  37.7 1.6 scatter_fusion
  43.8 2.7 and_reduce_fusion
  47.2 2.0 collective-permute-start.2
  49.2 1.5 collective-permute-start.3
  50.6 1.2 fusion.165
  52.2 1.1 collective-permute-done.3
  57.4 1.4 fusion.2
  59.9 1.5 reshape.500
  61.4 2.3 fusion.27
  66.5 2.7 broadcast_in_dim.52
  69.2 3.9 %reshape.503 = f32[48,44,140]{0,2,1:T(8,128)S(1)} reshape(f32[48,44,70,2]{0,3,2,1:T(2,128)} %broadcast_in_dim.52) | data formatting | bytes 2365440 | tf_op jit(solution)/shard_map/reshape | solution.py:316
  73.2 3.0 %copy.175 = f32[48,44,140]{2,0,1:T(8,128)} copy(f32[48,44,140]{0,2,1:T(8,128)S(1)} %reshape.503) | data formatting | bytes 2365440 | tf_op jit(solution)/shard_map/reshape | solution.py:316
  76.2 2.4 add_convert_fusion
  79.9 1.1 reshape.493
  81.7 4.5 %fusion.93 = f32[4,256,256]{2,1,0:T(8,128)S(1)} fusion(f32[4,2,256,256]{3,2,0,1:T(8,128)} %all-gather.2.cloned.1.call-done, f32[256,256]{1,0:T(8,128)S(1)} %get-tuple-element.345, f32[256,256]{1,0:T(8,128)S(1)} %get-tuple-element.344), kind=kOutput, calls=%fused_computation.132 | convolution fusion | flops 807075840 | bytes 3670016 | tf_op jit(solution)/shard_map/ab,nbc->nac/dot_general | solution.py:55
  86.2 2.7 fusion.6
  89.0 2.7 fusion.91
  91.6 3.1 %fusion.78 = f32[4,256,256]{2,1,0:T(8,128)S(1)} fusion(f32[4,256,256]{1,2,0:T(8,128)S(1)} %fusion.6), kind=kOutput, calls=%fused_computation.117 | convolution fusion | flops 806289408 | bytes 2097152 | tf_op jit(solution)/shard_map/nab,bc->nac/dot_general | solution.py:59
  94.7 2.7 fusion.89
  97.5 2.8 fusion.5
  100.2 2.7 convolution_subtract_fusion.2
  103.0 2.8 add_reduce_fusion.1
  106.6 2.8 fusion.45
  109.4 2.7 fusion.41
  112.1 2.7 fusion.4
  114.8 2.7 fusion.85
  117.5 2.9 %fusion.71 = f32[4,256,256]{2,1,0:T(8,128)S(1)} fusion(f32[4,256,256]{1,2,0:T(8,128)S(1)} %fusion.4), kind=kOutput, calls=%fused_computation.108 | convolution fusion | flops 806354944 | bytes 2097152 | tf_op jit(solution)/shard_map/nab,bc->nac/dot_general | solution.py:59
  120.5 2.7 fusion.3
  123.2 2.7 convolution_subtract_fusion
  125.9 2.9 %convert_reduce_fusion.1 = (f32[256,256]{1,0:T(8,128)S(1)}, f32[256,256]{1,0:T(8,128)S(1)}, f32[256,256]{1,0:T(8,128)S(1)}) fusion(f32[4,2,256,256]{3,2,0,1:T(8,128)S(1)} %copy-done.3, f32[4,256,256]{2,1,0:T(8,128)S(1)} %convolution_subtract_fusion, f32[4,256,256]{2,1,0:T(8,128)S(1)} %fusion.71, f32[4,256,256]{1,2,0:T(8,128)S(1)} %fusion.3), kind=kOutput, calls=%fused_computation.69 | convolution fusion | flops 810549248 | bytes 6029312 | tf_op jit(solution)/shard_map/nab,bc->nac/dot_general | solution.py:59
  129.5 3.0 %scatter.33 = f32[1,2,288,256]{3,2,1,0:T(8,128)S(1)} dynamic-update-slice(f32[1,2,288,256]{3,2,1,0:T(8,128)S(1)} %broadcast_in_dim.47, f32[1,2,256,256]{3,2,1,0:T(8,128)S(1)} %maximum_select_fusion, s32[]{:T(128)} %constant.234.clone.1, s32[]{:T(128)} %constant.234.clone.1, s32[]{:T(128)} %bitcast.46, s32[]{:T(128)} %constant.234.clone.1) | dynamic-update-slice | bytes 1048580 | tf_op jit(solution)/shard_map/vmap(vmap())/scatter | solution.py:260
  133.9 3.9 %scatter_fusion.1 = f32[8,2,8192]{2,1,0:T(2,128)} fusion(f32[8,2,8192]{2,1,0:T(2,128)} %broadcast_in_dim.42, s32[9]{0:T(128)S(1)} %fusion.165, f32[9,2,8192]{2,1,0:T(2,128)S(1)} %reshape.646), kind=kCustom, calls=%fused_computation.5 | custom fusion | bytes 1769508 | tf_op jit(solution)/shard_map/scatter | solution.py:266
  137.7 6.0 %all-to-all-start.1 = ((f32[8,1,2,8192]{3,2,1,0:T(2,128)}), f32[8,1,2,8192]{3,2,1,0:T(2,128)S(1)}, u32[]{:S(2)}, u32[]{:S(2)}) async-start(f32[8,1,2,8192]{3,2,1,0:T(2,128)} %bitcast.50), calls=%async_computation.1 | async-start | bytes 1048576 | tf_op jit(solution)/shard_map/all_to_all | solution.py:269
  145.9 12.1 %all-to-all-done.1 = f32[8,1,2,8192]{3,2,1,0:T(2,128)S(1)} async-done(((f32[8,1,2,8192]{3,2,1,0:T(2,128)}), f32[8,1,2,8192]{3,2,1,0:T(2,128)S(1)}, u32[]{:S(2)}, u32[]{:S(2)}) %all-to-all-start.1) | async-done | bytes 524320 | tf_op jit(solution)/shard_map/all_to_all | solution.py:269
  158.5 71.6 %while.21 = (s32[]{:T(128)}, f32[3,32,512]{2,1,0:T(8,128)S(1)}, s32[8]{0:T(128)S(1)}, s32[8]{0:T(128)S(1)}, f32[8,2,32,256]{3,2,1,0:T(8,128)S(1)}, /*index=5*/pr...) while((s32[]{:T(128)}, f32[3,32,512]{2,1,0:T(8,128)S(1)}, ...), condition=%wide.region_12.13_spmd, body=%wide.region_11.12_spmd.sunk | while | flops 49166 | bytes 491874 | solution.py:294
  230.1 7.5 %copy.199 = f32[3,32,512]{0,1,2:T(8,128)} copy(f32[3,32,512]{2,1,0:T(8,128)S(1)} %get-tuple-element.250) | data formatting | bytes 393216
  237.6 8.8 %reshape.694 = f32[512,96]{1,0:T(8,128)} reshape(f32[512,32,3]{2,1,0:T(8,128)} %bitcast.338) | data formatting | bytes 393216
  247.9 8.1 %psum.7 = f32[1]{0:T(128)} all-reduce(f32[1]{0:T(128)S(6)} %scatter.35), channel_id=1, replica_groups=mesh['tile'=8,'mode'=4] {'mode'}, use_global_device_ids=true, to_apply=%region_15.16 | all-reduce | flops 1 | bytes 8 | tf_op jit(solution)/shard_map/psum | solution.py:236
  256.0 10.4 %reduce-scatter.4.cloned.1.call-done = f32[128,96]{1,0:T(8,128)} async-done(((f32[512,96]{1,0:T(8,128)}), f32[128,96]{1,0:T(8,128)}) %reduce-scatter.4.cloned.1.call-update) | async-done | bytes 49168
  266.5 3.0 %reshape.695 = f32[128,32,3]{2,1,0:T(8,128)S(1)} reshape(f32[128,96]{1,0:T(8,128)} %reduce-scatter.4.cloned.1.call-done) | data formatting | bytes 98304
  269.5 1.9 slice_add_fusion
  271.4 2.7 copy.205
  274.1 1.4 copy.203
  (189 shorter events, 60.7 us)
Async XLA Ops:
  7.2 54.2 %copy-start = (bf16[4,48,48]{2,1,0:T(8,128)(2,1)S(1)}, bf16[4,48,48]{2,1,0:T(8,128)(2,1)}, u32[]{:S(2)}) copy-start(bf16[4,48,48]{2,1,0:T(8,128)(2,1)} %param.28) | copy-start | bytes 55300
  8.0 39.0 %collective-permute-start = (bf16[2,6,128]{2,0,1:T(2,128)(2,1)S(1)}, bf16[2,6,128]{2,0,1:T(2,128)(2,1)S(1)}, u32[]{:S(2)}, u32[]{:S(2)}) collective-permute-start(bf16[2,6,128]{2,0,1:T(2,128)(2,1)S(1)} %get-tuple-element.348), channel_id=1, source_target_pairs={{0,4},{4,8},{8,12},{12,16},{16,20},{20,24},{24,28},{1,5},{5,9},{9,... | collective-permute-start | bytes 9224 | tf_op jit(solution)/shard_map/ppermute | solution.py:22
  12.9 34.2 %collective-permute-start.1 = (bf16[2,6,128]{2,0,1:T(2,128)(2,1)S(1)}, bf16[2,6,128]{2,0,1:T(2,128)(2,1)S(1)}, u32[]{:S(2)}, u32[]{:S(2)}) collective-permute-start(bf16[2,6,128]{2,0,1:T(2,128)(2,1)S(1)} %get-tuple-element.349), channel_id=1, source_target_pairs={{4,0},{8,4},{12,8},{16,12},{20,16},{24,20},{28,24},{5,1},{9,5},{13... | collective-permute-start | bytes 9224 | tf_op jit(solution)/shard_map/ppermute | solution.py:23
  19.6 17.8 %copy-start.8 = (s32[8]{0:T(128)S(1)}, s32[8]{0:T(128)}, u32[]{:S(2)}) copy-start(s32[8]{0:T(128)} %param.25) | copy-start | bytes 100
  28.4 14.6 %copy-start.13 = (s32[1,3]{1,0:T(1,128)S(1)}, s32[1,3]{1,0:T(1,128)}, u32[]{:S(2)}) copy-start(s32[1,3]{1,0:T(1,128)} %constant.255.clone.1) | copy-start | bytes 40
  28.4 15.4 %copy-start.12 = (s32[4]{0:T(128)S(1)}, s32[4]{0:T(128)}, u32[]{:S(2)}) copy-start(s32[4]{0:T(128)} %constant.256.clone.1) | copy-start | bytes 52
  28.4 25.1 %copy-start.9 = (bf16[9,48,2]{1,2,0:T(2,128)(2,1)S(1)}, bf16[9,48,2]{1,2,0:T(2,128)(2,1)}, u32[]{:S(2)}) copy-start(bf16[9,48,2]{1,2,0:T(2,128)(2,1)} %param.26) | copy-start | bytes 5188
  29.7 50.2 %all-to-all-start = ((bf16[8,1,2,8192]{3,2,1,0:T(2,128)(2,1)}), bf16[8,1,2,8192]{3,2,1,0:T(2,128)(2,1)}, u32[]{:S(2)}, u32[]{:S(2)}) async-start(bf16[8,1,2,8192]{3,2,1,0:T(2,128)(2,1)} %reshape.693), calls=%async_computation | async-start | bytes 524288 | tf_op jit(solution)/shard_map/all_to_all | solution.py:199
  36.7 45.0 %all-gather.2.cloned.1.call-start = ((), (), s32[]{:S(2)}) async-start(), calls=%async_computation.3 | async-start | bytes 2621440 | tf_op jit(solution)/shard_map/all_gather | solution.py:169
  47.2 5.0 %collective-permute-start.2 = (bf16[2,44,6]{2,0,1:T(2,128)(2,1)S(1)}, bf16[2,44,6]{2,0,1:T(2,128)(2,1)S(1)}, u32[]{:S(2)}, u32[]{:S(2)}) collective-permute-start(bf16[2,44,6]{2,0,1:T(2,128)(2,1)S(1)} %get-tuple-element.346), channel_id=1, source_target_pairs={{0,1},{1,2},{2,3},{4,5},{5,6},{6,7},{8,9},{9,10},{10,11},{12,13},{... | collective-permute-start | bytes 3176 | tf_op jit(solution)/shard_map/ppermute | solution.py:22
  49.2 4.2 %collective-permute-start.3 = (bf16[2,44,6]{2,0,1:T(2,128)(2,1)S(1)}, bf16[2,44,6]{2,0,1:T(2,128)(2,1)S(1)}, u32[]{:S(2)}, u32[]{:S(2)}) collective-permute-start(bf16[2,44,6]{2,0,1:T(2,128)(2,1)S(1)} %get-tuple-element.347), channel_id=1, source_target_pairs={{1,0},{2,1},{3,2},{5,4},{6,5},{7,6},{9,8},{10,9},{11,10},{13,12},{... | collective-permute-start | bytes 3176 | tf_op jit(solution)/shard_map/ppermute | solution.py:23
  56.4 1.0 copy-start.11
  58.8 2.5 copy-start.2
  59.8 1.5 copy-start.15
  61.3 2.3 copy-start.7
  65.0 0.8 copy-start.10
  76.2 2.4 copy-start.14
  81.7 4.5 %copy-start.3 = (f32[4,2,256,256]{3,2,0,1:T(8,128)S(1)}, f32[4,2,256,256]{3,2,0,1:T(8,128)}, u32[]{:S(2)}) copy-start(f32[4,2,256,256]{3,2,0,1:T(8,128)} %all-gather.2.cloned.1.call-done) | copy-start | bytes 6291460
  103.0 2.8 copy-start.5
  137.7 20.3 %all-to-all-start.1 = ((f32[8,1,2,8192]{3,2,1,0:T(2,128)}), f32[8,1,2,8192]{3,2,1,0:T(2,128)S(1)}, u32[]{:S(2)}, u32[]{:S(2)}) async-start(f32[8,1,2,8192]{3,2,1,0:T(2,128)} %bitcast.50), calls=%async_computation.1 | async-start | bytes 1048576 | tf_op jit(solution)/shard_map/all_to_all | solution.py:269
  143.8 122.7 %reduce-scatter.4.cloned.1.call-start = ((), (), s32[]{:S(2)}) async-start(), calls=%async_computation.4 | async-start | bytes 327680
  237.6 9.7 %copy-start.16 = (f32[2]{0:T(128)S(1)}, f32[2]{0:T(128)}, u32[]{:S(2)}) copy-start(f32[2]{0:T(128)} %param.33) | copy-start | bytes 28
  269.5 8.0 %copy-start.1 = (bf16[4,48,48]{2,1,0:T(8,128)(2,1)S(1)}, bf16[4,48,48]{2,1,0:T(8,128)(2,1)}, u32[]{:S(2)}) copy-start(bf16[4,48,48]{2,1,0:T(8,128)(2,1)} %param.28) | copy-start | bytes 55300
  271.4 4.1 %copy-start.4 = (f32[2,32,128]{2,1,0:T(8,128)S(1)}, f32[2,32,128]{2,1,0:T(8,128)}, u32[]{:S(2)}) copy-start(f32[2,32,128]{2,1,0:T(8,128)} %param.20) | copy-start | bytes 98308
  271.4 4.1 %copy-start.6 = (f32[2,32,128]{2,1,0:T(8,128)S(1)}, f32[2,32,128]{2,1,0:T(8,128)}, u32[]{:S(2)}) copy-start(f32[2,32,128]{2,1,0:T(8,128)} %param.21) | copy-start | bytes 98308
Sparse Core Ops, SparseCore 0:
  39.1 24.3 all-gather.1
  246.5 19.8 reduce-scatter.3
where the time goes:
time: 290 us; the launch traced here: 285 us
  local copies, waits for them, and re-layouts  87.1 us (30%)
  matrix products  59.9 us (21%)
  loops' own time  41.9 us (14%)
  waiting for transfers between devices  24.4 us (8%)
  starting transfers between devices  22.9 us (8%)
  between operations  17.9 us (6%)
  other arithmetic  17.2 us (6%)
  blocking collectives  13.4 us (5%)
    another operation x1, loops' own time, per_device(): acc_rows = lax.fori_loop(0, slot_count, add_slot, start_acc)  41.9 us
    unnamed x42, local copies, waits for them, and re-layouts  25.3 us
    dot_general x8, matrix products, left_product(): jnp.einsum('ab,nbc->nac', table, values, precision=lax.Precision.HIGHEST)  23.6 us
    dot_general x8, matrix products, right_product(): jnp.einsum('nab,bc->nac', values, table, precision=lax.Precision.HIGHEST)  22.5 us
    all_to_all x1, waiting for transfers between devices, per_device(): lax.all_to_all(buffer.reshape(tile_count, pair_most, 2, rows_dev * patch)...  12.1 us
    dot_general x27, matrix products, conv_block(): jnp.einsum('oc,chw->ohw', weight[tap], window, preferred_element_type=jnp...  11.6 us
    unnamed x3, waiting for transfers between devices  11.1 us
    psum x1, blocking collectives, per_device(): misfit = lax.psum(misfit_local, 'mode')  8.15 us
  transfers between devices with their start and end apart: 8, of which 3 were waited for; matrix products, arithmetic and copies ran while one was open for 18% of the time, Pallas kernels for 0%

commit v1 on v0

--- a/solution.py
+++ b/solution.py
@@ -1,8 +1,12 @@
+import functools
 import math
 
 import jax
 import jax.numpy as jnp
+import numpy as np
 from jax import lax
+from jax.experimental import pallas as pl
+from jax.experimental.pallas import tpu as pltpu
 from jax.sharding import PartitionSpec as P
 
 HALO = 6
@@ -116,7 +120,7 @@
     return (jnp.minimum(send_table, pos_count - 1), send_table < pos_count)
 
 
-def per_device(
+def general_device(
     obj_x,
     dual_u,
     probes,
@@ -155,7 +159,8 @@
     indices = jnp.arange(pos_count, dtype=jnp.int32)
     touches = (first_strip <= tile_id) & (last_strip >= tile_id)
     is_mine = owner == tile_id
-    mine_rank = jnp.cumsum(is_mine.astype(jnp.int32)) - 1
+    up_to = is_mine[None, :] & (indices[None, :] <= indices[:, None])
+    mine_rank = jnp.sum(up_to.astype(jnp.int32), axis=1) - 1
     own_index = (
         jnp.full((own_most,), pos_count, jnp.int32)
         .at[jnp.where(is_mine, mine_rank, own_most)]
@@ -195,7 +200,7 @@
     def take(start):
         return lax.dynamic_slice_in_dim(strip_full, start, patch, 2)
 
-    cut = jax.vmap(take)(starts)
+    cut = lax.map(take, starts)
     arrived = lax.all_to_all(
         cut.reshape(tile_count, pair_most, 2, rows_dev * patch),
         "tile",
@@ -208,13 +213,19 @@
     offsets = plan[6]
     count = offsets.shape[0]
     blocks = arrived.reshape(tile_count, pair_most, 2, rows_dev, patch)
-    picked = blocks[strip_safe, rank_safe]
+    chosen = (strip_safe * pair_most + rank_safe).reshape(-1)
+    flat_blocks = blocks.reshape(slot_count, 2, rows_dev, patch)
+
+    def choose(slot):
+        return lax.dynamic_index_in_dim(flat_blocks, slot, 0, keepdims=False)
+
+    picked = lax.map(choose, chosen).reshape(count, strips_per, 2, rows_dev, patch)
     tall = jnp.transpose(picked, (0, 2, 1, 3, 4)).reshape(count, 2, strips_per * rows_dev, patch)
 
     def crop(block, offset):
         return lax.dynamic_slice_in_dim(block, offset, patch, 1)
 
-    patches = jax.vmap(crop)(tall, offsets)
+    patches = lax.map(lambda pair: crop(*pair), (tall, offsets))
     obj_re = patches[:, 0].astype(jnp.float32)[:, None]
     obj_im = patches[:, 1].astype(jnp.float32)[:, None]
     wave_re = (all_re[None] * obj_re - all_im[None] * obj_im).reshape(
@@ -323,6 +334,537 @@
     return (obj_next, aux_next, dual_next, misfit)
 
 
+def split_bf16(values):
+    high = values.astype(jnp.bfloat16)
+    low = (values - high.astype(jnp.float32)).astype(jnp.bfloat16)
+    return (high, low)
+
+
+def dot_f32(left, right):
+    return jnp.dot(left, right, preferred_element_type=jnp.float32)
+
+
+def dot_split(left, right):
+    return (
+        dot_f32(left[0], right[0]) + dot_f32(left[0], right[1]) + dot_f32(left[1], right[0])
+    )
+
+
+def table_parts(length):
+    grid = np.arange(length)[:, None] * np.arange(length)[None, :] % length
+    angle = 2.0 * np.pi / length * grid
+    cos = np.cos(angle) / math.sqrt(length)
+    sin = -np.sin(angle) / math.sqrt(length)
+    left = np.block([[cos, -sin], [sin, cos]]).astype(np.float32)
+    right = np.block([[cos, sin], [-sin, cos]]).astype(np.float32)
+    parts = []
+    for table in (left, right):
+        high = table.astype(jnp.bfloat16)
+        low = (table - high.astype(np.float32)).astype(jnp.bfloat16)
+        parts += [high, low]
+    return parts
+
+
+def tap_phases():
+    phases = np.zeros((9, 4, 9, 4), np.float32)
+    for tap in range(9):
+        for i in range(2):
+            for j in range(2):
+                a = i + tap // 3 - 1
+                b = j + tap % 3 - 1
+                s = (a // 2 + 1) * 3 + b // 2 + 1
+                phases[tap, 2 * i + j, s, a % 2 * 2 + b % 2] = 1.0
+    return phases
+
+
+MESH = pl.DeviceIdType.MESH
+
+
+def fast_kernel(
+    tiles,
+    modes,
+    corners,
+    owner,
+    b_out,
+    obj,
+    dual,
+    probes,
+    intensity,
+    left_hi,
+    left_lo,
+    right_hi,
+    right_lo,
+    w_in,
+    b_in,
+    w_down,
+    b_down,
+    w_mid,
+    b_mid,
+    w_out,
+    obj_next,
+    aux_next,
+    dual_next,
+    misfit,
+    gath,
+    ext,
+    pows,
+    pow_in,
+    planes,
+    phase_in,
+    phase_out,
+    conv,
+    far_s,
+    p1,
+    p1_in,
+    p2,
+    p2_in,
+    back_hi,
+    back_lo,
+    canvas,
+    c_in,
+    half,
+    half_in,
+    mine,
+    rows_in,
+    a_send,
+    a_recv,
+    b_send,
+    b_recv,
+    y_send,
+    y_recv,
+    f_send,
+    f_recv,
+    h_send,
+    h_recv,
+    w_send,
+    w_recv,
+    p1_send,
+    p1_recv,
+    p2_send,
+    p2_recv,
+    g1_send,
+    g1_recv,
+    g2_send,
+    g2_recv,
+    g3_send,
+    g3_recv,
+):
+    f32 = jnp.float32
+    bf16 = jnp.bfloat16
+    t = lax.axis_index("tile")
+    m = lax.axis_index("mode")
+    rows, cols = obj.shape[1], obj.shape[2]
+    patch = intensity.shape[1]
+    positions = owner.shape[0]
+    core = lax.rem(m, 2)
+    row = m // 2
+    mate = m + 1 - 2 * core
+    cross = lax.rem(m + 2, modes)
+    cross_mate = lax.rem(mate + 2, modes)
+    quarters = p1.shape[0]
+    part = patch // quarters
+    coarse_rows = rows // 2 + HALO
+    lanes = coarse_rows * cols
+    edge = (ext.shape[2] - rows) // 2
+
+    def around(index, step, count):
+        return lax.rem(index + step + count, count)
+
+    barrier = pltpu.get_barrier_semaphore()
+    greeted = [(around(t, d, tiles), m) for d in range(1, tiles)]
+    greeted += [(t, around(m, d, modes)) for d in range(1, modes)]
+    greeted += [(around(t, a, tiles), around(m, b, modes)) for a in (-1, 1) for b in (-1, 1)]
+    for who in greeted:
+        pl.semaphore_signal(barrier, inc=1, device_id=who, device_id_type=MESH)
+
+    gath[m, t] = obj[...].astype(bf16)
+    ext[1, :, edge : edge + rows, :] = (obj[...] + dual[...]).astype(bf16)
+    row_start = pl.multiple_of(t * rows, rows)
+    probe_re = probes[0, 0, pl.ds(row_start, rows), :]
+    probe_im = probes[0, 1, pl.ds(row_start, rows), :]
+    pows[...] = probe_re * probe_re + probe_im * probe_im
+
+    pl.semaphore_wait(barrier, len(greeted))
+
+    sent = []
+
+    def remote(source, target, send, recv, who):
+        return pltpu.make_async_remote_copy(
+            src_ref=source,
+            dst_ref=target,
+            send_sem=send,
+            recv_sem=recv,
+            device_id=who,
+            device_id_type=MESH,
+        )
+
+    def launch(*args):
+        copy = remote(*args)
+        copy.start()
+        sent.append(copy)
+        return copy
+
+    def block_copy(source):
+        return remote(gath.at[m, source], gath.at[m, source], a_send.at[0], a_recv.at[source], (t, mate))
+
+    halo = []
+    for a in (-1, 0, 1):
+        for b in (-1, 0, 1):
+            if a == 0 and b == 0:
+                continue
+            if a == 1:
+                source = ext.at[1, :, rows : rows + edge, :]
+                target = ext.at[1 - b, :, 0:edge, :]
+            elif a == -1:
+                source = ext.at[1, :, edge : 2 * edge, :]
+                target = ext.at[1 - b, :, edge + rows : 2 * edge + rows, :]
+            else:
+                source = ext.at[1, :, edge : edge + rows, :]
+                target = ext.at[1 - b, :, edge : edge + rows, :]
+            who = (around(t, a, tiles), around(m, b, modes))
+            number = len(halo)
+            halo.append(launch(source, target, h_send.at[number], h_recv.at[number], who))
+    for d in range(1, tiles):
+        launch(
+            gath.at[m, t], gath.at[m, t], a_send.at[d], a_recv.at[t], (around(t, d, tiles), m)
+        )
+
+    def spread(source):
+        block = gath.at[m, source]
+        near = launch(block, block, b_send.at[source], b_recv.at[source], (t, mate))
+        over = launch(block, block, y_send.at[source], y_recv.at[source], (t, cross))
+        return (near, over)
+
+    order = [around(t, d, tiles) for d in range(tiles)]
+    spreads = [spread(t)]
+    weights_in = []
+    for d in range(1, modes):
+        weights_in.append(
+            launch(
+                pows, pow_in.at[d - 1], w_send.at[d - 1], w_recv.at[d - 1], (t, around(m, d, modes))
+            )
+        )
+
+    for copy in halo:
+        copy.wait_recv()
+    line = lax.broadcasted_iota(jnp.int32, (cols, cols), 0)
+    place = lax.broadcasted_iota(jnp.int32, (cols, cols), 1)
+    wide = cols // 2 + HALO
+    for j in range(2):
+        plane = None
+        for b in range(3):
+            pick = (b * cols + line == cols - HALO + j + 2 * place) & (place < wide)
+            block = ext[b].reshape(-1, cols)
+            term = dot_f32(block, pick.astype(f32).astype(bf16))
+            plane = term if plane is None else plane + term
+        planes[2 * j : 2 * j + 2] = plane.reshape(2, -1, cols)
+    for y in range(coarse_rows):
+        first = edge - HALO + 2 * y
+        phase_in[0:4, y * cols : (y + 1) * cols] = planes[:, first, :]
+        phase_in[4:8, y * cols : (y + 1) * cols] = planes[:, first + 1, :]
+    spot = lax.broadcasted_iota(jnp.int32, (1, lanes), 1)
+    coarse_y = t * (rows // 2) - HALO // 2 + spot // cols
+    coarse_x = m * (cols // 2) - HALO // 2 + spot % cols
+    inside = (coarse_y >= 0) & (coarse_y < tiles * rows // 2)
+    inside = inside & (coarse_x >= 0) & (coarse_x < modes * cols // 2) & (spot % cols < wide)
+    mask = inside.astype(f32)
+
+    def moved(value, s):
+        offset = (s // 3 - 1) * cols + s % 3 - 1
+        return value if offset == 0 else pltpu.roll(value, (-offset) % lanes, 1)
+
+    inputs = phase_in[...] * mask
+    stacked = jnp.concatenate([moved(inputs, s) for s in range(9)], axis=0).astype(bf16)
+    first_map = jnp.maximum(dot_f32(w_in[...], stacked) + b_in[...], 0.0).astype(bf16)
+    second_map = jnp.maximum(dot_f32(w_down[...], first_map) + b_down[...], 0.0) * mask
+
+    for d in range(1, tiles):
+        block_copy(order[d]).wait_recv()
+        spreads.append(spread(order[d]))
+
+    second_map = second_map.astype(bf16).astype(f32)
+    stacked = jnp.concatenate([moved(second_map, s).astype(bf16) for s in range(9)], axis=0)
+    third_map = jnp.maximum(dot_f32(w_mid[...], stacked) + b_mid[...], 0.0)
+    third_map = third_map.astype(bf16).astype(f32)
+
+    forwards = []
+    for d in range(tiles):
+        spreads[d][1].wait_recv()
+        block = gath.at[cross, order[d]]
+        forwards.append(launch(block, block, f_send.at[order[d]], f_recv.at[order[d]], (t, mate)))
+
+    fourth_map = (
+        (jnp.concatenate([third_map] * 4, axis=0) + first_map.astype(f32)) * mask
+    ).astype(bf16)
+    shares = dot_f32(w_out[...], fourth_map)
+    total = None
+    for s in range(9):
+        term = moved(shares[8 * s : 8 * s + 8], s)
+        total = term if total is None else total + term
+    margin = HALO // 2
+    for y in range(rows // 2):
+        phase_out[:, y, :] = total[:, (y + margin) * cols : (y + margin + 1) * cols]
+    for i in range(2):
+        merged = None
+        for j in range(2):
+            pick = (place == 2 * (line - margin) + j).astype(f32).astype(bf16)
+            value = phase_out[4 * i + 2 * j : 4 * i + 2 * j + 2].reshape(rows, cols)
+            high, low = split_bf16(value)
+            term = dot_f32(high, pick) + dot_f32(low, pick)
+            merged = term if merged is None else merged + term
+        for o in range(2):
+            conv[o, pl.ds(i, rows // 2, stride=2), :] = merged[
+                o * (rows // 2) : (o + 1) * (rows // 2)
+            ]
+    for o in range(2):
+        aux_next[o] = obj[o] + dual[o] - (conv[o] + b_out[o])
+
+    for copy in weights_in:
+        copy.wait_recv()
+    probe_power = pows[...]
+    for d in range(1, modes):
+        probe_power = probe_power + pow_in[d - 1]
+    shift = (
+        m * cols
+        + lax.broadcasted_iota(jnp.int32, (patch, cols), 1)
+        - lax.broadcasted_iota(jnp.int32, (patch, cols), 0)
+    )
+    times = jnp.zeros((patch, cols), f32)
+    col = jnp.int32(0)
+    for k in range(positions):
+        times = times + (shift == corners[1, k]).astype(f32)
+        col = col + jnp.where(owner[k] == t, corners[1, k], 0)
+    times = times.astype(bf16)
+    high, low = split_bf16(probe_power)
+    denom = dot_f32(high, times) + dot_f32(low, times)
+
+    window = (
+        lax.broadcasted_iota(jnp.int32, (patch, modes * cols), 1)
+        == lax.broadcasted_iota(jnp.int32, (patch, modes * cols), 0) + col
+    )
+    window = window.astype(f32).astype(bf16)
+    for d in range(tiles):
+        spreads[d][0].wait_recv()
+        forwards[d].wait_recv()
+    cut = []
+    for plane in range(2):
+        value = None
+        for b in range(modes):
+            block = gath[b, :, plane].reshape(patch, cols)
+            term = lax.dot_general(
+                block,
+                window[:, b * cols : (b + 1) * cols],
+                (((1,), (1,)), ((), ())),
+                preferred_element_type=f32,
+            )
+            value = term if value is None else value + term
+        cut.append(value)
+    wave = jnp.concatenate(
+        [
+            probes[0, 0] * cut[0] - probes[0, 1] * cut[1],
+            probes[0, 0] * cut[1] + probes[0, 1] * cut[0],
+        ],
+        axis=0,
+    )
+    side = dot_split((left_hi[...], left_lo[...]), split_bf16(wave))
+    side = split_bf16(jnp.concatenate([side[:patch], side[patch:]], axis=1))
+    right = (right_hi[...], right_lo[...])
+    left = (left_hi[...], left_lo[...])
+    near = []
+    for q in range(quarters):
+        at = slice(q * part, (q + 1) * part)
+        far = dot_split((side[0][at], side[1][at]), right)
+        far_s[at] = far
+        p1[q] = (far[:, :patch] * far[:, :patch] + far[:, patch:] * far[:, patch:]).astype(bf16)
+        near.append(launch(p1.at[q], p1_in.at[q], p1_send.at[q], p1_recv.at[q], (t, mate)))
+    over = []
+    for q in range(quarters):
+        near[q].wait_recv()
+        p2[q] = (p1[q].astype(f32) + p1_in[q].astype(f32)).astype(bf16)
+        over.append(launch(p2.at[q], p2_in.at[q], p2_send.at[q], p2_recv.at[q], (t, cross)))
+    errors = jnp.zeros((part, patch), f32)
+    for q in range(quarters):
+        at = slice(q * part, (q + 1) * part)
+        over[q].wait_recv()
+        power = p2[q].astype(f32) + p2_in[q].astype(f32)
+        measured = jnp.sqrt(intensity[0, at])
+        gap = jnp.sqrt(power) - measured
+        errors = errors + gap * gap
+        scale = measured * lax.rsqrt(jnp.maximum(power, floor_level))
+        scaled = far_s[at] * jnp.concatenate([scale, scale], axis=1)
+        back = dot_split(split_bf16(scaled), left)
+        for plane in range(2):
+            high, low = split_bf16(back[:, plane * patch : (plane + 1) * patch])
+            to = slice(plane * patch + q * part, plane * patch + (q + 1) * part)
+            back_hi[to] = high
+            back_lo[to] = low
+    misfit[0] = jnp.sum(errors) * (1.0 / (patch * patch))
+
+    back = (back_hi[...], back_lo[...])
+    near = []
+    for q in range(quarters):
+        at = slice(q * part, (q + 1) * part)
+        below = slice(patch + q * part, patch + (q + 1) * part)
+        value_re = dot_split((right_hi[at], right_lo[at]), back)
+        value_im = dot_split((right_hi[below], right_lo[below]), back)
+        re = probes[0, 0, at]
+        im = probes[0, 1, at]
+        grad = jnp.concatenate(
+            [re * value_re + im * value_im, re * value_im - im * value_re], axis=0
+        ).astype(bf16)
+        spread_out = dot_f32(grad, window).astype(bf16)
+        for b in range(modes):
+            canvas[q, b % 2, b // 2] = spread_out[:, b * cols : (b + 1) * cols]
+        near.append(
+            launch(
+                canvas.at[q, 1 - core], c_in.at[q], g1_send.at[q], g1_recv.at[q], (t, mate)
+            )
+        )
+    over = []
+    for q in range(quarters):
+        near[q].wait_recv()
+        half[q] = (
+            canvas[q, core, 1 - row].astype(f32) + c_in[q, 1 - row].astype(f32)
+        ).astype(bf16)
+        over.append(launch(half.at[q], half_in.at[q], g2_send.at[q], g2_recv.at[q], (t, cross)))
+    for q in range(quarters):
+        over[q].wait_recv()
+        value = (
+            canvas[q, core, row].astype(f32) + c_in[q, row].astype(f32) + half_in[q].astype(f32)
+        ).astype(bf16)
+        for u in range(part // rows):
+            for plane in range(2):
+                mine[q * (part // rows) + u, plane] = value[
+                    plane * part + u * rows : plane * part + (u + 1) * rows
+                ]
+    for d in range(1, tiles):
+        launch(
+            mine.at[order[d]], rows_in.at[t], g3_send.at[d], g3_recv.at[t], (order[d], m)
+        )
+    numer = mine[t].astype(f32)
+    for d in range(1, tiles):
+        remote(
+            mine.at[order[d]], rows_in.at[order[d]], g3_send.at[d], g3_recv.at[order[d]], (order[d], m)
+        ).wait_recv()
+        numer = numer + rows_in[order[d]].astype(f32)
+    scale = 1.0 / (denom + rho_weight)
+    for o in range(2):
+        value = (numer[o] + rho_weight * (aux_next[o] - dual[o])) * scale
+        obj_next[o] = value
+        dual_next[o] = dual[o] + value - aux_next[o]
+    for copy in sent:
+        copy.wait_send()
+
+
+def fast_device(
+    obj_x,
+    dual_u,
+    probes,
+    intensity,
+    corners,
+    owner,
+    w_in,
+    b_in,
+    w_down,
+    b_down,
+    w_mid,
+    b_mid,
+    w_out,
+    b_out,
+):
+    tiles = lax.axis_size("tile")
+    modes = lax.axis_size("mode")
+    rows, cols = obj_x.shape[1], obj_x.shape[2]
+    patch = probes.shape[-1]
+    chans = w_in.shape[1]
+    phases = jnp.asarray(tap_phases(), jnp.bfloat16)
+    big_in = jnp.einsum("tasp,toc->aospc", phases, w_in).reshape(4 * chans, 72)
+    big_out = jnp.einsum("tasp,toc->saopc", phases, w_out).reshape(72, 4 * chans)
+    big_down = jnp.transpose(w_down, (1, 0, 2)).reshape(chans, 4 * chans)
+    big_mid = jnp.transpose(w_mid, (1, 0, 2)).reshape(chans, 9 * chans)
+    f32 = jnp.float32
+    bf16 = jnp.bfloat16
+    vmem = pl.BlockSpec(memory_space=pltpu.VMEM)
+    smem = pl.BlockSpec(memory_space=pltpu.SMEM)
+    quarters = 4
+    part = patch // quarters
+    edge = 16
+    coarse = rows // 2 + HALO
+    dma = pltpu.SemaphoreType.DMA
+    block = jax.ShapeDtypeStruct((2, rows, cols), f32)
+    return pl.pallas_call(
+        functools.partial(fast_kernel, tiles, modes),
+        out_shape=(block, block, block, jax.ShapeDtypeStruct((1,), f32)),
+        in_specs=[smem] * 3 + [vmem] * 15,
+        out_specs=(vmem, vmem, vmem, smem),
+        scratch_shapes=[
+            pltpu.VMEM((modes, tiles, 2, rows, cols), bf16),
+            pltpu.VMEM((3, 2, rows + 2 * edge, cols), bf16),
+            pltpu.VMEM((rows, patch), f32),
+            pltpu.VMEM((modes - 1, rows, patch), f32),
+            pltpu.VMEM((4, rows + 2 * edge, cols), f32),
+            pltpu.VMEM((8, coarse * cols), f32),
+            pltpu.VMEM((8, rows // 2, cols), f32),
+            pltpu.VMEM((2, rows, cols), f32),
+            pltpu.VMEM((patch, 2 * patch), f32),
+            pltpu.VMEM((quarters, part, patch), bf16),
+            pltpu.VMEM((quarters, part, patch), bf16),
+            pltpu.VMEM((quarters, part, patch), bf16),
+            pltpu.VMEM((quarters, part, patch), bf16),
+            pltpu.VMEM((2 * patch, patch), bf16),
+            pltpu.VMEM((2 * patch, patch), bf16),
+            pltpu.VMEM((quarters, 2, modes // 2, 2 * part, cols), bf16),
+            pltpu.VMEM((quarters, modes // 2, 2 * part, cols), bf16),
+            pltpu.VMEM((quarters, 2 * part, cols), bf16),
+            pltpu.VMEM((quarters, 2 * part, cols), bf16),
+            pltpu.VMEM((tiles, 2, rows, cols), bf16),
+            pltpu.VMEM((tiles, 2, rows, cols), bf16),
+        ]
+        + [dma((tiles,))] * 8
+        + [dma((8,))] * 2
+        + [dma((modes - 1,))] * 2
+        + [dma((quarters,))] * 8
+        + [dma((tiles,))] * 2,
+        compiler_params=pltpu.CompilerParams(
+            collective_id=0, has_side_effects=True, vmem_limit_bytes=40 * 1024 * 1024
+        ),
+    )(
+        corners,
+        owner,
+        b_out,
+        obj_x,
+        dual_u,
+        probes,
+        intensity,
+        *[jnp.asarray(part_of) for part_of in table_parts(patch)],
+        big_in,
+        jnp.tile(b_in, 4)[:, None],
+        big_down,
+        b_down[:, None],
+        big_mid,
+        b_mid[:, None],
+        big_out,
+    )
+
+
+def per_device(obj_x, dual_u, probes, intensity, corners, owner, *weights):
+    tiles = lax.axis_size("tile")
+    modes = lax.axis_size("mode")
+    fits = (
+        obj_x.shape[1] * tiles == probes.shape[-1]
+        and intensity.shape[0] == 1
+        and owner.shape[0] == tiles
+        and modes == 4
+        and tiles > 2
+        and probes.shape[0] == 1
+        and obj_x.shape[1] % 32 == 0
+        and obj_x.shape[2] % 128 == 0
+        and probes.shape[-1] // 4 % obj_x.shape[1] == 0
+    )
+    run = fast_device if fits else general_device
+    return run(obj_x, dual_u, probes, intensity, corners, owner, *weights)
+
+
 def solution(mesh):
     return jax.shard_map(
         per_device,

time: 290 us -> 53.9 us (0.19); the launches traced: 285 us -> 53.3 us
  local copies, waits for them, and re-layouts: 87.1 us -> 9.49 us
  matrix products: 59.9 us -> 2.09 us
  loops' own time: 41.9 us -> 0 us
  Pallas kernels: 0 us -> 39.1 us
  waiting for transfers between devices: 24.4 us -> 0 us
  starting transfers between devices: 22.9 us -> 0 us
  other arithmetic: 17.2 us -> 0 us
  between operations: 17.9 us -> 2.61 us
  blocking collectives: 13.4 us -> 0 us
    dot_general x44 -> x2, matrix products: 59.9 us -> 2.09 us  [the longest x1 1.06 us: fast_device(): jnp.einsum('tasp,toc->saopc', phases, w_out).reshape(72, 4 * chans)]
    another operation x1 -> x0, loops' own time: 41.9 us -> none  [per_device(): acc_rows = lax.fori_loop(0, slot_count, add_slot, start_acc)]
    pallas_call x0 -> x1, Pallas kernels: none -> 39.1 us  [fast_device(): pl.pallas_call(functools.partial(fast_kernel, tiles, modes), out_shape=(b...]
    dynamic_slice x32 -> x0, local copies, waits for them, and re-layouts: 18.8 us -> none  [the longest x8 4.72 us: add_slot(): alive = slot_live[slot_no].astype(jnp.float32)]
    unnamed x42 -> x35, local copies, waits for them, and re-layouts: 25.3 us -> 6.73 us
    all_to_all x2 -> x0, starting transfers between devices: 13 us -> none  [the longest x1 6.96 us: per_device(): lax.all_to_all(cut.reshape(tile_count, pair_most, 2, rows_dev * patch), '...]
    all_to_all x2 -> x0, waiting for transfers between devices: 12.1 us -> none  [the longest x1 12.1 us: per_device(): lax.all_to_all(buffer.reshape(tile_count, pair_most, 2, rows_dev * patch)...]
    reshape x8 -> x5, local copies, waits for them, and re-layouts: 11.7 us -> 0.51 us  [the longest x2 0.21 us: fast_device(): big_in = jnp.einsum('tasp,toc->aospc', phases, w_in).reshape(4 * chans, 72)]
  transfers between devices with their start and end apart: 8 -> 0, of which waited for: 3 -> 0; matrix products, arithmetic and copies ran while one was open for 18% -> 0% of each run, Pallas kernels for 0% -> 0%
where the time goes in v1:
time: 53.9 us; the launch traced here: 53.3 us
  Pallas kernels  39.1 us (73%)
  local copies, waits for them, and re-layouts  9.49 us (18%)
  between operations  2.61 us (5%)
  matrix products  2.09 us (4%)
    pallas_call x1, Pallas kernels, fast_device(): pl.pallas_call(functools.partial(fast_kernel, tiles, modes), out_shape=(b...  39.1 us
    unnamed x35, local copies, waits for them, and re-layouts  6.73 us

profile of v1, /device:TPU:0, one launch (start us, length us, event | category | flops | bytes accessed | tf_op | source)
XLA Modules:
  0.0 53.3 jit_solution(9703029866575966903)
XLA Ops:
  0.6 0.0 copy-start
  0.6 0.7 %copy-done = bf16[9,48,2]{1,2,0:T(2,128)(2,1)S(1)} copy-done((bf16[9,48,2]{1,2,0:T(2,128)(2,1)S(1)}, bf16[9,48,2]{1,2,0:T(2,128)(2,1)}, u32[]{:S(2)}) %copy-start) | copy-done | bytes 1752
  1.3 0.0 copy-start.12
  1.3 0.0 copy-start.6
  1.3 1.0 %convolution_bitcast_fusion.1 = bf16[4,48,9,4,2]{1,2,4,3,0:T(8,128)(2,1)S(1)} fusion(bf16[9,4,9,4,1]{0,2,4,3,1:T(8,128)(2,1)} %constant.17, bf16[9,48,2,1,1]{1,2,0,4,3:T(2,128)(2,1)S(1)} %bitcast.18), kind=kOutput, calls=%fused_computation.1 | convolution fusion | flops 248832 | bytes 31968 | tf_op jit(solution)/shard_map/tasp,toc->aospc/dot_general | solution.py:781
  2.4 0.0 copy-start.3
  2.4 0.1 copy.32
  2.5 0.1 reshape.21
  2.6 0.1 copy.37.w_in
  2.7 0.0 copy-done.12
  2.7 0.0 copy-start.13
  2.7 0.0 copy-start.14
  2.7 0.0 copy-start.15
  2.7 0.0 copy-start.2
  2.7 1.1 %convolution_bitcast_fusion = bf16[9,4,2,4,48]{4,0,2,3,1:T(8,128)(2,1)S(1)} fusion(bf16[9,4,9,4,1]{0,2,4,3,1:T(8,128)(2,1)} %constant.17, bf16[9,2,48,1,1]{2,1,0,4,3:T(2,128)(2,1)S(1)} %bitcast.22), kind=kOutput, calls=%fused_computation | convolution fusion | flops 248832 | bytes 31968 | tf_op jit(solution)/shard_map/tasp,toc->saopc/dot_general | solution.py:782
  3.8 0.0 copy-start.1
  3.9 0.1 reshape.24.w_out
  4.0 1.0 %copy.34 = bf16[48,9,48]{0,2,1:T(8,128)(2,1)S(1)} copy(bf16[48,9,48]{2,0,1:T(8,128)(2,1)} %bitcast.20) | data formatting | bytes 82944 | tf_op jit(solution)/shard_map/transpose | solution.py:784
  5.0 0.1 copy.40.w_mid
  5.1 0.0 copy-done.13
  5.1 0.1 broadcast_in_dim_tile.4.b_in
  5.2 0.8 %copy.33 = bf16[48,4,48]{2,1,0:T(4,128)(2,1)S(1)} copy(bf16[48,4,48]{2,0,1:T(8,128)(2,1)} %bitcast.21) | data formatting | bytes 36864 | tf_op jit(solution)/shard_map/transpose | solution.py:783
  6.1 0.1 reshape.22.w_down
  6.2 0.0 copy-done.14
  6.2 0.1 copy.39.b_down
  6.3 0.0 copy-done.15
  6.3 0.0 copy-start.9
  6.3 0.0 copy-start.10
  6.3 0.0 copy-start.11
  6.3 0.1 copy.41.b_mid
  6.4 0.0 copy-done.6
  6.4 0.0 copy-done.3
  6.4 0.0 copy-done.2
  6.4 0.0 copy-done.1
  6.4 0.5 %copy-done.9 = s32[2,8]{1,0:T(2,128)S(1)} copy-done((s32[2,8]{1,0:T(2,128)S(1)}, s32[2,8]{1,0:T(2,128)}, u32[]{:S(2)}) %copy-start.9) | copy-done | bytes 88
  7.0 0.0 copy-done.10
  7.0 0.0 copy-done.11
  7.0 0.0 copy-start.4
  7.0 1.0 %copy-done.4 = bf16[512,512]{1,0:T(8,128)(2,1)S(1)} copy-done((bf16[512,512]{1,0:T(8,128)(2,1)S(1)}, bf16[512,512]{1,0:T(8,128)(2,1)}, u32[]{:S(2)}) %copy-start.4) | copy-done | bytes 524312
  8.0 0.0 copy-start.5
  8.0 1.0 %copy-done.5 = bf16[512,512]{1,0:T(8,128)(2,1)S(1)} copy-done((bf16[512,512]{1,0:T(8,128)(2,1)S(1)}, bf16[512,512]{1,0:T(8,128)(2,1)}, u32[]{:S(2)}) %copy-start.5) | copy-done | bytes 524312
  9.1 0.0 copy-start.7
  9.1 0.8 %copy-done.7 = f32[2,32,128]{2,1,0:T(8,128)S(1)} copy-done((f32[2,32,128]{2,1,0:T(8,128)S(1)}, f32[2,32,128]{2,1,0:T(8,128)}, u32[]{:S(2)}) %copy-start.7) | copy-done | bytes 32792
  9.8 0.8 %copy-done.8 = f32[2,32,128]{2,1,0:T(8,128)S(1)} copy-done((f32[2,32,128]{2,1,0:T(8,128)S(1)}, f32[2,32,128]{2,1,0:T(8,128)}, u32[]{:S(2)}) %copy-start.8) | copy-done | bytes 32792
  10.6 39.1 %shard_map.210 = (f32[2,32,128]{2,1,0:T(8,128)S(1)}, f32[2,32,128]{2,1,0:T(8,128)S(1)}, f32[2,32,128]{2,1,0:T(8,128)S(1)}, f32[1]{0:T(128)}) custom-call(s32[2,8]{1,0:T(2,128)S(1)} %copy-done.9, s32[8]{0:T(128)S(1)} %copy-done.10, f32[2]{0:T(128)S(1)} %copy-done.11, f32[2,32,128]{2,1,0:T(8,128)S(1)} %copy-done.7, f32[2,32,128]{2,1,0:T(8,128)S(1)} %copy-done.8, ...), custom_call_target="tpu_custom_call" | custom-call | tf_op jit(solution)/shard_map/pallas_call | solution.py:795
  49.7 0.6 %copy.57 = f32[2,32,128]{2,1,0:T(8,128)} copy(f32[2,32,128]{2,1,0:T(8,128)S(1)} %get-tuple-element.8) | data formatting | bytes 65536
  50.3 0.6 %copy.58 = f32[2,32,128]{2,1,0:T(8,128)} copy(f32[2,32,128]{2,1,0:T(8,128)S(1)} %get-tuple-element.9) | data formatting | bytes 65536
  50.9 0.6 %copy.59 = f32[2,32,128]{2,1,0:T(8,128)} copy(f32[2,32,128]{2,1,0:T(8,128)S(1)} %get-tuple-element.10) | data formatting | bytes 65536
  (3 shorter events, 0.0 us)
Async XLA Ops:
  0.6 0.7 %copy-start = (bf16[9,48,2]{1,2,0:T(2,128)(2,1)S(1)}, bf16[9,48,2]{1,2,0:T(2,128)(2,1)}, u32[]{:S(2)}) copy-start(bf16[9,48,2]{1,2,0:T(2,128)(2,1)} %param.25) | copy-start | bytes 5188
  1.3 1.4 %copy-start.12 = (bf16[9,2,48]{2,1,0:T(2,128)(2,1)S(1)}, bf16[9,2,48]{2,1,0:T(2,128)(2,1)}, u32[]{:S(2)}) copy-start(bf16[9,2,48]{2,1,0:T(2,128)(2,1)} %param.31) | copy-start | bytes 5188
  1.3 5.1 %copy-start.6 = (f32[1,256,256]{2,1,0:T(8,128)S(1)}, f32[1,256,256]{2,1,0:T(8,128)}, u32[]{:S(2)}) copy-start(f32[1,256,256]{2,1,0:T(8,128)} %intensity.1) | copy-start | bytes 786436
  2.4 4.0 %copy-start.3 = (bf16[512,512]{1,0:T(8,128)(2,1)S(1)}, bf16[512,512]{1,0:T(8,128)(2,1)}, u32[]{:S(2)}) copy-start(bf16[512,512]{1,0:T(8,128)(2,1)} %constant.12.clone.left_lo) | copy-start | bytes 1572868
  2.7 2.4 %copy-start.13 = (f32[48]{0:T(128)S(1)}, f32[48]{0:T(128)}, u32[]{:S(2)}) copy-start(f32[48]{0:T(128)} %param.26) | copy-start | bytes 580
  2.7 3.5 %copy-start.14 = (f32[48]{0:T(128)S(1)}, f32[48]{0:T(128)}, u32[]{:S(2)}) copy-start(f32[48]{0:T(128)} %param.28) | copy-start | bytes 580
  2.7 3.6 %copy-start.15 = (f32[48]{0:T(128)S(1)}, f32[48]{0:T(128)}, u32[]{:S(2)}) copy-start(f32[48]{0:T(128)} %param.30) | copy-start | bytes 580
  2.7 3.7 %copy-start.2 = (bf16[512,512]{1,0:T(8,128)(2,1)S(1)}, bf16[512,512]{1,0:T(8,128)(2,1)}, u32[]{:S(2)}) copy-start(bf16[512,512]{1,0:T(8,128)(2,1)} %constant.11.clone.left_hi) | copy-start | bytes 1572868
  3.8 2.6 %copy-start.1 = (f32[1,2,256,256]{3,2,1,0:T(8,128)S(1)}, f32[1,2,256,256]{3,2,1,0:T(8,128)}, u32[]{:S(2)}) copy-start(f32[1,2,256,256]{3,2,1,0:T(8,128)} %probes.1) | copy-start | bytes 1572868
  6.3 0.7 %copy-start.9 = (s32[2,8]{1,0:T(2,128)S(1)}, s32[2,8]{1,0:T(2,128)}, u32[]{:S(2)}) copy-start(s32[2,8]{1,0:T(2,128)} %corners.1) | copy-start | bytes 196
  6.3 0.7 %copy-start.10 = (s32[8]{0:T(128)S(1)}, s32[8]{0:T(128)}, u32[]{:S(2)}) copy-start(s32[8]{0:T(128)} %owner.1) | copy-start | bytes 100
  6.3 0.7 %copy-start.11 = (f32[2]{0:T(128)S(1)}, f32[2]{0:T(128)}, u32[]{:S(2)}) copy-start(f32[2]{0:T(128)} %b_out.1) | copy-start | bytes 28
  7.0 1.0 %copy-start.4 = (bf16[512,512]{1,0:T(8,128)(2,1)S(1)}, bf16[512,512]{1,0:T(8,128)(2,1)}, u32[]{:S(2)}) copy-start(bf16[512,512]{1,0:T(8,128)(2,1)} %constant.13.clone.right_hi) | copy-start | bytes 1572868
  8.0 1.0 %copy-start.5 = (bf16[512,512]{1,0:T(8,128)(2,1)S(1)}, bf16[512,512]{1,0:T(8,128)(2,1)}, u32[]{:S(2)}) copy-start(bf16[512,512]{1,0:T(8,128)(2,1)} %constant.14.clone.right_lo) | copy-start | bytes 1572868
  9.1 0.8 %copy-start.7 = (f32[2,32,128]{2,1,0:T(8,128)S(1)}, f32[2,32,128]{2,1,0:T(8,128)}, u32[]{:S(2)}) copy-start(f32[2,32,128]{2,1,0:T(8,128)} %obj.1) | copy-start | bytes 98308
  9.8 0.8 %copy-start.8 = (f32[2,32,128]{2,1,0:T(8,128)S(1)}, f32[2,32,128]{2,1,0:T(8,128)}, u32[]{:S(2)}) copy-start(f32[2,32,128]{2,1,0:T(8,128)} %dual.1) | copy-start | bytes 98308
